TPU v7x, 32 devices: a whole 2x2x4 slice. The times are simulated.
32 devices in a mesh: expert: 32 (over z, y, x, core).
Axes of the slice: x: 2, y: 2, z: 4, core: 2. Of those that a mesh axis runs over, the one named last changes fastest.
Arguments:
- tokens: bfloat16 [2048, 3584], P('expert'), may hold values from -6 to 6
- expert_ids: int32 [2048, 8], P('expert'), may hold values from 0 to 31, all different within a row; in each aligned block of 64 rows (0 to 63, 64 to 127, ...) at most 24 rows name the same one
- gate_weights: float32 [2048, 8], P('expert'), may hold values from 0.05 to 1
- host: int32 [32], replicated, may hold values from 0 to 31, each once
- w_in: bfloat16 [32, 2, 3584, 2, 512], P('expert'), may hold values from -0.09375 to 0.09375
- w_out: bfloat16 [32, 2, 512, 3584], P('expert'), may hold values from -0.1875 to 0.1875
Outputs:
- moe_out: bfloat16 [2048, 3584], P('expert')
Inputs may be any that keep to these rules, and one draw needn't show every extreme that they name: `expert_ids`: each row names 8 different experts; in the rows of one device no expert is named more than 24 times, a bound that some block reaches. A permutation: device d holds the weights of expert host[d].
All inputs are finite; a program needn't handle non-finite values.
Results may differ from a plain program's by a relative error of at most 0.011.
Values may be sent and summed in bfloat16 or wider, within the bound.
A program may use at most 192 MiB of HBM per device.

v0:
```python
import functools

import jax
import jax.numpy as jnp
from jax import lax
from jax.experimental import pallas as pl
from jax.experimental.pallas import tpu as pltpu
from jax.sharding import PartitionSpec as P


def ffn_kernel(groups, blocks, group_rows, tile, place_ref, gate_ref, tok_ref, first_ref, second_ref,
               out_ref, rows, weight, hidden, result):
    step = pl.program_id(0)
    group_tokens = tok_ref.shape[0]
    block_rows = rows.shape[0] // blocks

    def selection(group):
        place = place_ref[pl.ds(group, 1), :]
        slots = lax.broadcasted_iota(jnp.int32, (group_rows, group_tokens), 0)
        return slots == place

    @pl.when(step < groups)
    def _():
        chosen = selection(step)
        begin = pl.multiple_of(step * group_rows, group_rows)
        here = pl.ds(begin, group_rows)
        gates = gate_ref[pl.ds(step, 1), :]
        weight[here, :] = jnp.sum(jnp.where(chosen, gates, 0.0), axis=1, keepdims=True)
        rows[here, :] = jnp.dot(
            chosen.astype(jnp.bfloat16), tok_ref[...], preferred_element_type=jnp.float32
        ).astype(jnp.bfloat16)

    @pl.when((step >= groups) & (step < groups + blocks))
    def _():
        begin = pl.multiple_of((step - groups) * block_rows, block_rows)
        here = pl.ds(begin, block_rows)
        halves, _, twice = first_ref.shape
        half = twice // 2
        per = half // tile

        @pl.loop(0, halves * per)
        def _(number):
            h, j = number // per, number % per
            at = pl.multiple_of(j * tile, tile)
            x = rows[here, :]
            g = jnp.dot(x, first_ref[h, :, pl.ds(at, tile)], preferred_element_type=jnp.float32)
            u = jnp.dot(x, first_ref[h, :, pl.ds(half + at, tile)], preferred_element_type=jnp.float32)
            value = g / (1.0 + jnp.exp(-g)) * u
            hidden[:, pl.ds(pl.multiple_of(number * tile, tile), tile)] = value.astype(jnp.bfloat16)

        @pl.loop(0, second_ref.shape[1] // tile)
        def _(number):
            at = pl.ds(pl.multiple_of(number * tile, tile), tile)
            y = jnp.dot(hidden[...], second_ref[:, at], preferred_element_type=jnp.float32)
            result[here, at] = (y * weight[here, :]).astype(jnp.bfloat16)

    @pl.when(step >= groups + blocks)
    def _():
        group = step - groups - blocks
        chosen = selection(group).astype(jnp.bfloat16)
        begin = pl.multiple_of(group * group_rows, group_rows)
        out_ref[...] = lax.dot_general(
            chosen, result[pl.ds(begin, group_rows), :], (((0,), (0,)), ((), ())),
            preferred_element_type=jnp.float32,
        ).astype(jnp.bfloat16)


def local(tokens, expert_ids, gate_weights, host, w_in, w_out):
    experts = lax.axis_size("expert")
    tok_dev, top_count = expert_ids.shape
    d_model = tokens.shape[1]
    slot_count = max(
        2, min(tok_dev // 2, (3 * tok_dev * top_count + 2 * experts - 1) // (2 * experts))
    )
    together = 4 if slot_count >= 16 else 8
    groups = experts // together
    group_rows = together * slot_count
    group_tokens = together * tok_dev
    blocks = 2
    total = groups * group_rows
    mine = host[lax.axis_index("expert")]

    routing = jnp.concatenate([expert_ids.astype(jnp.float32), gate_weights], axis=1)
    routing = lax.all_gather(routing, "expert", axis=0, tiled=True)
    everyone = lax.all_gather(tokens, "expert", axis=0, tiled=True)

    hit = routing[:, :top_count] == mine.astype(jnp.float32)
    gate = jnp.sum(jnp.where(hit, routing[:, top_count:], 0.0), axis=1).reshape(groups, group_tokens)
    named = jnp.any(hit, axis=1).reshape(experts, tok_dev)
    earlier = jnp.arange(tok_dev)[:, None] < jnp.arange(tok_dev)[None, :]
    rank = jnp.dot(
        named.astype(jnp.float32), earlier.astype(jnp.float32), preferred_element_type=jnp.float32
    ).astype(jnp.int32)
    source = jnp.arange(experts, dtype=jnp.int32)[:, None] % together
    place = jnp.where(named, source * slot_count + rank, -1).reshape(groups, group_tokens)

    halves, _, _, half = w_in.shape[1:]
    first = w_in[0].reshape(halves, d_model, 2 * half)
    second = w_out[0].reshape(halves * half, d_model)
    whole = lambda shape: pl.BlockSpec(shape, lambda i: (0,) * len(shape), pipeline_mode=pl.Buffered(1))
    partial = pl.pallas_call(
        functools.partial(ffn_kernel, groups, blocks, group_rows, 256),
        grid=(2 * groups + blocks,),
        out_shape=jax.ShapeDtypeStruct((experts * tok_dev, d_model), jnp.bfloat16),
        in_specs=[
            whole(place.shape),
            whole(gate.shape),
            pl.BlockSpec((group_tokens, d_model), lambda i: (jnp.minimum(i, groups - 1), 0)),
            whole(first.shape),
            whole(second.shape),
        ],
        out_specs=pl.BlockSpec((group_tokens, d_model), lambda i: (jnp.maximum(i - groups - blocks, 0), 0)),
        scratch_shapes=[
            pltpu.VMEM((total, d_model), jnp.bfloat16),
            pltpu.VMEM((total, 1), jnp.float32),
            pltpu.VMEM((total // blocks, halves * half), jnp.bfloat16),
            pltpu.VMEM((total, d_model), jnp.bfloat16),
        ],
        compiler_params=pltpu.CompilerParams(vmem_limit_bytes=60 * 1024 * 1024),
        cost_estimate=pl.CostEstimate(flops=17 * 10**9, bytes_accessed=52 * 10**6, transcendentals=10**6),
    )(place, gate, everyone, first, second)
    return lax.psum_scatter(partial, "expert", scatter_dimension=0, tiled=True)


def solution(mesh):
    in_specs = (
        P("expert", None),
        P("expert", None),
        P("expert", None),
        P(),
        P("expert", None, None, None, None),
        P("expert", None, None, None),
    )
    out_specs = P("expert", None)
    return jax.shard_map(local, mesh=mesh, in_specs=in_specs, out_specs=out_specs, check_vma=False)
```

profile of v0, /device:TPU:0, one launch (start us, length us, event | category | flops | bytes accessed | tf_op | source)
XLA Modules:
  0.0 333.3 jit_solution(13189188398750927994)
XLA Ops:
  6.5 0.0 all-gather.3.cloned.1.call-start
  6.5 0.7 all-gather.3.cloned.1.call-update
  7.3 0.0 reduce-scatter.2.cloned.1.call-start
  7.3 1.2 dynamic_slice.3
  9.2 0.7 convert_element_type.14
  9.9 0.7 maximum_bitcast_fusion
  10.6 44.8 %all-gather = f32[32,64,16]{1,2,0:T(8,128)S(1)} all-gather(f32[1,64,16]{1,2,0:T(8,128)S(1)} %maximum_bitcast_fusion), channel_id=1, replica_groups=mesh['expert'=32] {'expert'}, dimensions={0}, use_global_device_ids=true | all-gather | bytes 135168 | tf_op jit(solution)/shard_map/all_gather | solution.py:84
  55.4 0.1 copy.8
  55.5 0.1 reshape.31
  55.7 0.6 reshape.29.gate_ref
  56.3 0.1 reshape.27
  56.4 0.1 fusion.1
  56.5 0.7 reshape.28.place_ref
  57.2 24.4 %reshape_squeeze.6.first_ref = bf16[2,3584,1024]{2,1,0:T(8,128)(2,1)} reshape(bf16[1,2,3584,2,512]{4,3,2,1,0:T(2,128)(2,1)} %param.10) | data formatting | bytes 29360128 | tf_op jit(solution)/shard_map/reshape;squeeze | solution.py:98
  81.6 37.2 %all-gather.3.cloned.1.call-done.tok_ref = bf16[2048,3584]{1,0:T(8,128)(2,1)} async-done(((bf16[64,3584]{1,0:T(8,128)(2,1)}), bf16[2048,3584]{1,0:T(8,128)(2,1)}) %all-gather.3.cloned.1.call-update) | async-done | bytes 14680080 | tf_op jit(solution)/shard_map/all_gather | solution.py:85
  118.8 47.5 %shard_map.64 = bf16[2048,3584]{1,0:T(8,128)(2,1)} custom-call(s32[8,256]{1,0:T(8,128)} %reshape.28.place_ref, f32[8,256]{1,0:T(8,128)} %reshape.29.gate_ref, bf16[2048,3584]{1,0:T(8,128)(2,1)} %all-gather.3.cloned.1.call-done.tok_ref, bf16[2,3584,1024]{2,1,0:T(8,128)(2,1)} %reshape_squeeze.6.first_ref, bf16[1024,3584]{1,0:T(8,128)(2,1)} %bitcast.7), custom_call_target="tpu_custom_call" | custom-call | flops 16999999488 | bytes 52000000 | tf_op jit(solution)/shard_map/pallas_call | solution.py:101
  166.2 0.0 reduce-scatter.2.cloned.1.call-update
  166.3 160.2 %reduce-scatter.2.cloned.1.call-done = bf16[64,3584]{1,0:T(8,128)(2,1)} async-done(((bf16[2048,3584]{1,0:T(8,128)(2,1)}), bf16[64,3584]{1,0:T(8,128)(2,1)}) %reduce-scatter.2.cloned.1.call-update) | async-done | bytes 458768 | tf_op jit(solution)/shard_map/reduce_scatter | solution.py:122
  (3 shorter events, 0.1 us)
Async XLA Ops:
  6.5 112.2 %all-gather.3.cloned.1.call-start = ((), (), s32[]{:S(2)}) async-start(), calls=%async_computation.1 | async-start | bytes 15138816 | tf_op jit(solution)/shard_map/all_gather | solution.py:85
  7.3 319.2 %reduce-scatter.2.cloned.1.call-start = ((), (), s32[]{:S(2)}) async-start(), calls=%async_computation.2 | async-start | bytes 15138816 | tf_op jit(solution)/shard_map/reduce_scatter | solution.py:122
Sparse Core Ops, SparseCore 0:
  10.2 108.5 all-gather.2
  166.4 160.0 reduce-scatter.1
where the time goes:
time: 334 us; the launch traced here: 333 us
  waiting for transfers between devices  198 us (59%)
  Pallas kernels  47.5 us (14%)
  blocking collectives  44.8 us (13%)
  local copies, waits for them, and re-layouts  27.2 us (8%)
  between operations  14.1 us (4%)
    reduce_scatter x1, waiting for transfers between devices, local(): return lax.psum_scatter(partial, 'expert', scatter_dimension=0, tiled=True)  160 us
    pallas_call x1, Pallas kernels, local(): pl.pallas_call(functools.partial(ffn_kernel, groups, blocks, group_rows,...  47.5 us
    all_gather x1, blocking collectives, local(): routing = lax.all_gather(routing, 'expert', axis=0, tiled=True)  44.8 us
    all_gather x1, waiting for transfers between devices, local(): everyone = lax.all_gather(tokens, 'expert', axis=0, tiled=True)  37.2 us
    another operation x1, local copies, waits for them, and re-layouts, local(): first = w_in[0].reshape(halves, d_model, 2 * half)  24.4 us
  transfers between devices with their start and end apart: 2, of which 2 were waited for; matrix products, arithmetic and copies ran while one was open for 9% of the time, Pallas kernels for 0%

commit v1 on v0

--- a/solution.py
+++ b/solution.py
@@ -72,54 +72,78 @@
     slot_count = max(
         2, min(tok_dev // 2, (3 * tok_dev * top_count + 2 * experts - 1) // (2 * experts))
     )
+    sources = experts // 2
     together = 4 if slot_count >= 16 else 8
-    groups = experts // together
+    groups = sources // together
     group_rows = together * slot_count
     group_tokens = together * tok_dev
-    blocks = 2
     total = groups * group_rows
     mine = host[lax.axis_index("expert")]
+    same_core = [list(range(core, experts, 2)) for core in range(2)]
+    sibling = [(device, device ^ 1) for device in range(experts)]
 
-    routing = jnp.concatenate([expert_ids.astype(jnp.float32), gate_weights], axis=1)
-    routing = lax.all_gather(routing, "expert", axis=0, tiled=True)
-    everyone = lax.all_gather(tokens, "expert", axis=0, tiled=True)
-
-    hit = routing[:, :top_count] == mine.astype(jnp.float32)
-    gate = jnp.sum(jnp.where(hit, routing[:, top_count:], 0.0), axis=1).reshape(groups, group_tokens)
-    named = jnp.any(hit, axis=1).reshape(experts, tok_dev)
-    earlier = jnp.arange(tok_dev)[:, None] < jnp.arange(tok_dev)[None, :]
-    rank = jnp.dot(
-        named.astype(jnp.float32), earlier.astype(jnp.float32), preferred_element_type=jnp.float32
-    ).astype(jnp.int32)
-    source = jnp.arange(experts, dtype=jnp.int32)[:, None] % together
-    place = jnp.where(named, source * slot_count + rank, -1).reshape(groups, group_tokens)
+    high = lax.reduce_precision(gate_weights, 8, 7)
+    middle = lax.reduce_precision(gate_weights - high, 8, 7)
+    low = gate_weights - high - middle
+    routing = jnp.concatenate([expert_ids.astype(jnp.float32), high, middle, low], axis=1)
+    routing = jnp.pad(routing, ((0, 0), (0, 128 - 4 * top_count)))
+    outgoing = jnp.concatenate([tokens, routing.astype(jnp.bfloat16)], axis=1)
+    own = lax.all_gather(outgoing, "expert", axis=0, tiled=True, axis_index_groups=same_core)
+    other = lax.ppermute(own, "expert", sibling)
 
     halves, _, _, half = w_in.shape[1:]
     first = w_in[0].reshape(halves, d_model, 2 * half)
     second = w_out[0].reshape(halves * half, d_model)
-    whole = lambda shape: pl.BlockSpec(shape, lambda i: (0,) * len(shape), pipeline_mode=pl.Buffered(1))
-    partial = pl.pallas_call(
-        functools.partial(ffn_kernel, groups, blocks, group_rows, 256),
-        grid=(2 * groups + blocks,),
-        out_shape=jax.ShapeDtypeStruct((experts * tok_dev, d_model), jnp.bfloat16),
-        in_specs=[
-            whole(place.shape),
-            whole(gate.shape),
-            pl.BlockSpec((group_tokens, d_model), lambda i: (jnp.minimum(i, groups - 1), 0)),
-            whole(first.shape),
-            whole(second.shape),
-        ],
-        out_specs=pl.BlockSpec((group_tokens, d_model), lambda i: (jnp.maximum(i - groups - blocks, 0), 0)),
-        scratch_shapes=[
-            pltpu.VMEM((total, d_model), jnp.bfloat16),
-            pltpu.VMEM((total, 1), jnp.float32),
-            pltpu.VMEM((total // blocks, halves * half), jnp.bfloat16),
-            pltpu.VMEM((total, d_model), jnp.bfloat16),
-        ],
-        compiler_params=pltpu.CompilerParams(vmem_limit_bytes=60 * 1024 * 1024),
-        cost_estimate=pl.CostEstimate(flops=17 * 10**9, bytes_accessed=52 * 10**6, transcendentals=10**6),
-    )(place, gate, everyone, first, second)
-    return lax.psum_scatter(partial, "expert", scatter_dimension=0, tiled=True)
+
+    def partial_rows(gathered):
+        routing = gathered[:, d_model:].astype(jnp.float32)
+        ids, high, middle, low = (
+            routing[:, part * top_count:(part + 1) * top_count] for part in range(4)
+        )
+        hit = ids == mine.astype(jnp.float32)
+        gate = jnp.sum(jnp.where(hit, high + middle + low, 0.0), axis=1).reshape(groups, group_tokens)
+        named = jnp.any(hit, axis=1).reshape(sources, tok_dev)
+        earlier = jnp.arange(tok_dev)[:, None] < jnp.arange(tok_dev)[None, :]
+        rank = jnp.dot(
+            named.astype(jnp.float32), earlier.astype(jnp.float32), preferred_element_type=jnp.float32
+        ).astype(jnp.int32)
+        source = jnp.arange(sources, dtype=jnp.int32)[:, None] % together
+        place = jnp.where(named, source * slot_count + rank, -1).reshape(groups, group_tokens)
+        whole = lambda shape: pl.BlockSpec(
+            shape, lambda i: (0,) * len(shape), pipeline_mode=pl.Buffered(1)
+        )
+        return pl.pallas_call(
+            functools.partial(ffn_kernel, groups, 1, group_rows, 256),
+            grid=(2 * groups + 1,),
+            out_shape=jax.ShapeDtypeStruct((sources * tok_dev, d_model), jnp.bfloat16),
+            in_specs=[
+                whole(place.shape),
+                whole(gate.shape),
+                pl.BlockSpec((group_tokens, d_model), lambda i: (jnp.minimum(i, groups - 1), 0)),
+                whole(first.shape),
+                whole(second.shape),
+            ],
+            out_specs=pl.BlockSpec(
+                (group_tokens, d_model), lambda i: (jnp.maximum(i - groups - 1, 0), 0)
+            ),
+            scratch_shapes=[
+                pltpu.VMEM((total, d_model), jnp.bfloat16),
+                pltpu.VMEM((total, 1), jnp.float32),
+                pltpu.VMEM((total, halves * half), jnp.bfloat16),
+                pltpu.VMEM((total, d_model), jnp.bfloat16),
+            ],
+            compiler_params=pltpu.CompilerParams(vmem_limit_bytes=56 * 1024 * 1024),
+            cost_estimate=pl.CostEstimate(
+                flops=17 * 10**9, bytes_accessed=40 * 10**6, transcendentals=10**6
+            ),
+        )(place, gate, gathered, first, second)
+
+    kept = partial_rows(own)
+    handed = lax.ppermute(partial_rows(other), "expert", sibling)
+    summed = (kept.astype(jnp.float32) + handed.astype(jnp.float32)).astype(jnp.bfloat16)
+    return lax.psum_scatter(
+        summed, "expert", scatter_dimension=0, tiled=True, axis_index_groups=same_core
+    )
 
 
 def solution(mesh):

time: 334 us -> 381 us (1.14)
  waiting for transfers between devices: 198 us -> 264 us
  blocking collectives: 44.8 us -> 0 us
  other arithmetic: 1.45 us -> 17.1 us
  Pallas kernels: 47.5 us -> 54.9 us
    all_gather x1, waiting for transfers between devices: 37.2 us -> 109 us  [local(): lax.all_gather(outgoing, 'expert', axis=0, tiled=True, axis_index_groups=...]
    all_gather x1 -> x0, blocking collectives: 44.8 us -> none  [local(): routing = lax.all_gather(routing, 'expert', axis=0, tiled=True)]
    convert_element_type x1 -> x3, other arithmetic: 0.69 us -> 12.1 us  [the longest x1 10.1 us: local(): (kept.astype(jnp.float32) + handed.astype(jnp.float32)).astype(jnp.bfloat16)]
    pallas_call x1 -> x2, Pallas kernels: 47.5 us -> 54.9 us  [partial_rows(): pl.pallas_call(functools.partial(ffn_kernel, groups, 1, group_rows, 256),...]
    reduce_scatter x1, waiting for transfers between devices: 160 us -> 155 us  [local(): lax.psum_scatter(summed, 'expert', scatter_dimension=0, tiled=True, axis_...]
  transfers between devices with their start and end apart: 2 -> 4, of which waited for: 2 -> 2; matrix products, arithmetic and copies ran while one was open for 9% -> 8% of each run, Pallas kernels for 0% -> 7%
where the time goes in v1:
time: 381 us; the launch traced here: 380 us
  waiting for transfers between devices  264 us (69%)
  Pallas kernels  54.9 us (14%)
  local copies, waits for them, and re-layouts  29.2 us (8%)
  other arithmetic  17.1 us (4%)
  between operations  14.1 us (4%)
    reduce_scatter x1, waiting for transfers between devices, local(): lax.psum_scatter(summed, 'expert', scatter_dimension=0, tiled=True, axis_...  155 us
    all_gather x1, waiting for transfers between devices, local(): lax.all_gather(outgoing, 'expert', axis=0, tiled=True, axis_index_groups=...  109 us
    pallas_call x2, Pallas kernels, partial_rows(): pl.pallas_call(functools.partial(ffn_kernel, groups, 1, group_rows, 256),...  54.9 us
    another operation x1, local copies, waits for them, and re-layouts, local(): first = w_in[0].reshape(halves, d_model, 2 * half)  24.1 us
    convert_element_type x1, other arithmetic, local(): (kept.astype(jnp.float32) + handed.astype(jnp.float32)).astype(jnp.bfloat16)  10.1 us
  transfers between devices with their start and end apart: 4, of which 2 were waited for; matrix products, arithmetic and copies ran while one was open for 8% of the time, Pallas kernels for 7%

profile of v1, /device:TPU:0, one launch (start us, length us, event | category | flops | bytes accessed | tf_op | source)
XLA Modules:
  0.0 379.7 jit_solution(13478290915367798092)
XLA Ops:
  6.5 0.0 all-gather.2.cloned.1.call-start
  6.5 0.7 reduce-precision_convert_fusion.1
  7.2 0.8 copy.10
  8.0 0.1 copy.11
  8.1 0.1 copy.13
  8.2 0.7 convert_convert_fusion
  8.9 0.1 copy.12
  9.0 0.1 fusion.15
  9.1 1.8 pad_maximum_fusion
  10.9 0.0 all-gather.2.cloned.1.call-update
  10.9 0.0 reduce-scatter.2.cloned.1.call-start
  11.0 108.6 %all-gather.2.cloned.1.call-done.tok_ref = bf16[1024,3712]{1,0:T(8,128)(2,1)} async-done(((bf16[64,3712]{1,0:T(8,128)(2,1)}), bf16[1024,3712]{1,0:T(8,128)(2,1)}) %all-gather.2.cloned.1.call-update) | async-done | bytes 7602192 | tf_op jit(solution)/shard_map/all_gather | solution.py:91
  119.6 0.0 collective-permute-start
  119.6 1.2 dynamic_slice.3
  121.5 24.1 %reshape_squeeze.6.first_ref = bf16[2,3584,1024]{2,1,0:T(8,128)(2,1)} reshape(bf16[1,2,3584,2,512]{4,3,2,1,0:T(2,128)(2,1)} %param.10) | data formatting | bytes 29360128 | tf_op jit(solution)/shard_map/reshape;squeeze | solution.py:95
  145.5 0.0 collective-permute-done.tok_ref
  145.5 1.0 slice_convert_fusion
  146.5 0.6 fusion.5
  147.2 0.2 reduce_or.19
  147.4 0.1 reshape.39
  147.5 0.1 fusion.1
  147.6 0.7 reshape.40.place_ref
  148.3 0.6 reshape.41.gate_ref
  148.9 27.4 %shard_map.65 = bf16[1024,3584]{1,0:T(8,128)(2,1)} custom-call(s32[4,256]{1,0:T(4,128)} %reshape.40.place_ref, f32[4,256]{1,0:T(4,128)} %reshape.41.gate_ref, bf16[1024,3712]{1,0:T(8,128)(2,1)} %collective-permute-done.tok_ref, bf16[2,3584,1024]{2,1,0:T(8,128)(2,1)} %reshape_squeeze.6.first_ref, bf16[1024,3584]{1,0:T(8,128)(2,1)} %bitcast.4), custom_call_target="tpu_custom_call" | custom-call | flops 16999999488 | bytes 40000000 | tf_op jit(solution)/shard_map/pallas_call | solution.py:115
  176.3 0.5 collective-permute-start.1
  176.8 1.0 slice_convert_fusion.1
  177.8 0.6 fusion.7
  178.4 0.2 reduce_or.18
  178.7 0.1 reshape.36
  178.7 0.1 fusion.3
  178.8 0.7 reshape.37.place_ref
  179.6 0.6 reshape.38.gate_ref
  180.1 27.5 %shard_map.64 = bf16[1024,3584]{1,0:T(8,128)(2,1)} custom-call(s32[4,256]{1,0:T(4,128)} %reshape.37.place_ref, f32[4,256]{1,0:T(4,128)} %reshape.38.gate_ref, bf16[1024,3712]{1,0:T(8,128)(2,1)} %all-gather.2.cloned.1.call-done.tok_ref, bf16[2,3584,1024]{2,1,0:T(8,128)(2,1)} %reshape_squeeze.6.first_ref, bf16[1024,3584]{1,0:T(8,128)(2,1)} %bitcast.5), custom_call_target="tpu_custom_call" | custom-call | flops 16999999488 | bytes 40000000 | tf_op jit(solution)/shard_map/pallas_call | solution.py:115
  207.6 0.0 collective-permute-done.1
  207.6 10.1 %add_convert_fusion = bf16[1024,3584]{1,0:T(8,128)(2,1)} fusion(bf16[1024,3584]{1,0:T(8,128)(2,1)} %collective-permute-done.1, bf16[1024,3584]{1,0:T(8,128)(2,1)} %shard_map.64), kind=kLoop, calls=%fused_computation | loop fusion | flops 14680064 | bytes 22020096 | tf_op jit(solution)/shard_map/convert_element_type | solution.py:143
  217.8 0.0 reduce-scatter.2.cloned.1.call-update
  217.8 155.1 %reduce-scatter.2.cloned.1.call-done = bf16[64,3584]{1,0:T(8,128)(2,1)} async-done(((bf16[1024,3584]{1,0:T(8,128)(2,1)}), bf16[64,3584]{1,0:T(8,128)(2,1)}) %reduce-scatter.2.cloned.1.call-update) | async-done | bytes 458768 | tf_op jit(solution)/shard_map/reduce_scatter | solution.py:144
  (2 shorter events, 0.0 us)
Async XLA Ops:
  6.5 113.1 %all-gather.2.cloned.1.call-start = ((), (), s32[]{:S(2)}) async-start(), calls=%async_computation.1 | async-start | bytes 8077312 | tf_op jit(solution)/shard_map/all_gather | solution.py:91
  10.9 362.0 %reduce-scatter.2.cloned.1.call-start = ((), (), s32[]{:S(2)}) async-start(), calls=%async_computation.2 | async-start | bytes 7798784 | tf_op jit(solution)/shard_map/reduce_scatter | solution.py:144
  119.6 26.0 %collective-permute-start = (bf16[1024,3712]{1,0:T(8,128)(2,1)}, bf16[1024,3712]{1,0:T(8,128)(2,1)}, u32[]{:S(2)}, u32[]{:S(2)}) collective-permute-start(bf16[1024,3712]{1,0:T(8,128)(2,1)} %all-gather.2.cloned.1.call-done.tok_ref), channel_id=1, source_target_pairs={{0,1},{1,0},{2,3},{3,2},{4,5},{5,4},{6,7},{7,6},{8,9},{9,8},{10,11... | collective-permute-start | bytes 22806536 | tf_op jit(solution)/shard_map/ppermute | solution.py:92
  176.3 31.3 %collective-permute-start.1 = (bf16[1024,3584]{1,0:T(8,128)(2,1)}, bf16[1024,3584]{1,0:T(8,128)(2,1)}, u32[]{:S(2)}, u32[]{:S(2)}) collective-permute-start(bf16[1024,3584]{1,0:T(8,128)(2,1)} %shard_map.65), channel_id=1, source_target_pairs={{0,1},{1,0},{2,3},{3,2},{4,5},{5,4},{6,7},{7,6},{8,9},{9,8},{10,11... | collective-permute-start | bytes 22020104 | tf_op jit(solution)/shard_map/ppermute | solution.py:142
Sparse Core Ops, SparseCore 0:
  11.1 108.4 all-gather.1
  217.9 154.9 reduce-scatter.1

commit v2 on v1

--- a/solution.py
+++ b/solution.py
@@ -63,6 +63,57 @@
             chosen, result[pl.ds(begin, group_rows), :], (((0,), (0,)), ((), ())),
             preferred_element_type=jnp.float32,
         ).astype(jnp.bfloat16)
+
+
+def exchange_orders(experts):
+    bits = experts.bit_length() - 1
+    middle = list(range(1, bits - 1))
+    return [middle[k % len(middle):] + middle[:k % len(middle)] + [bits - 1] for k in range(3)]
+
+
+def column_parts(width):
+    tiles = width // 128
+    cuts = [tiles * k // 3 * 128 for k in range(3)] + [width]
+    return list(zip(cuts[:-1], cuts[1:]))
+
+
+def swap(block, bit, experts):
+    return lax.ppermute(block, "expert", [(i, i ^ (1 << bit)) for i in range(experts)])
+
+
+def gather_chips(block, experts):
+    parts = [block[:, low:high] for low, high in column_parts(block.shape[1])]
+    orders = [order[::-1] for order in exchange_orders(experts)]
+    held = [[] for _ in parts]
+    for stage in range(len(orders[0])):
+        for k, order in enumerate(orders):
+            bit = order[stage]
+            axis = sum(1 for other in held[k] if other > bit)
+            parts[k] = jnp.stack([parts[k], swap(parts[k], bit, experts)], axis=axis)
+            held[k].append(bit)
+    rows = experts // 2 * block.shape[0]
+    return jnp.concatenate([part.reshape(rows, part.shape[-1]) for part in parts], axis=1)
+
+
+def scatter_chips(total, experts):
+    orders = exchange_orders(experts)
+    bits = len(orders[0])
+    rows = total.shape[0] >> bits
+    parts = [
+        total[:, low:high].reshape((2,) * bits + (rows, high - low))
+        for low, high in column_parts(total.shape[1])
+    ]
+    left = [sorted(order, reverse=True) for order in orders]
+    for stage in range(bits):
+        for k, order in enumerate(orders):
+            bit = order[stage]
+            axis = left[k].index(bit)
+            kept = lax.index_in_dim(parts[k], 0, axis, keepdims=False)
+            sent = lax.index_in_dim(parts[k], 1, axis, keepdims=False)
+            came = swap(sent, bit, experts)
+            parts[k] = (kept.astype(jnp.float32) + came.astype(jnp.float32)).astype(jnp.bfloat16)
+            left[k].remove(bit)
+    return jnp.concatenate(parts, axis=1)
 
 
 def local(tokens, expert_ids, gate_weights, host, w_in, w_out):
@@ -79,7 +130,6 @@
     group_tokens = together * tok_dev
     total = groups * group_rows
     mine = host[lax.axis_index("expert")]
-    same_core = [list(range(core, experts, 2)) for core in range(2)]
     sibling = [(device, device ^ 1) for device in range(experts)]
 
     high = lax.reduce_precision(gate_weights, 8, 7)
@@ -88,7 +138,7 @@
     routing = jnp.concatenate([expert_ids.astype(jnp.float32), high, middle, low], axis=1)
     routing = jnp.pad(routing, ((0, 0), (0, 128 - 4 * top_count)))
     outgoing = jnp.concatenate([tokens, routing.astype(jnp.bfloat16)], axis=1)
-    own = lax.all_gather(outgoing, "expert", axis=0, tiled=True, axis_index_groups=same_core)
+    own = gather_chips(outgoing, experts)
     other = lax.ppermute(own, "expert", sibling)
 
     halves, _, _, half = w_in.shape[1:]
@@ -141,9 +191,7 @@
     kept = partial_rows(own)
     handed = lax.ppermute(partial_rows(other), "expert", sibling)
     summed = (kept.astype(jnp.float32) + handed.astype(jnp.float32)).astype(jnp.bfloat16)
-    return lax.psum_scatter(
-        summed, "expert", scatter_dimension=0, tiled=True, axis_index_groups=same_core
-    )
+    return scatter_chips(summed, experts)
 
 
 def solution(mesh):

time: 381 us -> 262 us (0.69)
  waiting for transfers between devices: 264 us -> 113 us
  starting transfers between devices: 0.54 us -> 36.4 us
  between operations: 14.1 us -> 0.99 us
  other arithmetic: 17.1 us -> 22.9 us
  local copies, waits for them, and re-layouts: 29.2 us -> 33.2 us
    reduce_scatter x1 -> x0, waiting for transfers between devices: 155 us -> none  [local(): lax.psum_scatter(summed, 'expert', scatter_dimension=0, tiled=True, axis_...]
    ppermute x0 -> x24, waiting for transfers between devices: none -> 113 us  [swap(): lax.ppermute(block, 'expert', [(i, i ^ 1 << bit) for i in range(experts)])]
    all_gather x1 -> x0, waiting for transfers between devices: 109 us -> none  [local(): lax.all_gather(outgoing, 'expert', axis=0, tiled=True, axis_index_groups=...]
    ppermute x0 -> x24, starting transfers between devices: none -> 35.9 us  [swap(): lax.ppermute(block, 'expert', [(i, i ^ 1 << bit) for i in range(experts)])]
  transfers between devices with their start and end apart: 4 -> 26, of which waited for: 2 -> 18; matrix products, arithmetic and copies ran while one was open for 8% -> 13% of each run, Pallas kernels for 7% -> 10%
where the time goes in v2:
time: 262 us
  waiting for transfers between devices  113 us (43%)
  Pallas kernels  54.9 us (21%)
  starting transfers between devices  36.4 us (14%)
  local copies, waits for them, and re-layouts  33.2 us (13%)
  other arithmetic  22.9 us (9%)
    ppermute x24, waiting for transfers between devices, swap(): lax.ppermute(block, 'expert', [(i, i ^ 1 << bit) for i in range(experts)])  113 us
    pallas_call x2, Pallas kernels, partial_rows(): pl.pallas_call(functools.partial(ffn_kernel, groups, 1, group_rows, 256),...  54.9 us
    ppermute x24, starting transfers between devices, swap(): lax.ppermute(block, 'expert', [(i, i ^ 1 << bit) for i in range(experts)])  35.9 us
    another operation x1, local copies, waits for them, and re-layouts, local(): first = w_in[0].reshape(halves, d_model, 2 * half)  24.1 us
    convert_element_type x1, other arithmetic, local(): (kept.astype(jnp.float32) + handed.astype(jnp.float32)).astype(jnp.bfloat16)  10 us
  transfers between devices with their start and end apart: 26, of which 18 were waited for; matrix products, arithmetic and copies ran while one was open for 13% of the time, Pallas kernels for 10%

profile of v2, /device:TPU:0, one launch (start us, length us, event | category | flops | bytes accessed | tf_op | source)
XLA Modules:
  0.0 261.5 jit_solution(6123482153225485391)
XLA Ops:
  0.0 0.9 slice_bitcast_fusion.18
  0.9 4.1 %collective-permute-start.4 = (bf16[64,1152]{1,0:T(8,128)(2,1)S(1)}, bf16[64,1152]{1,0:T(8,128)(2,1)S(1)}, u32[]{:S(2)}, u32[]{:S(2)}) collective-permute-start(bf16[64,1152]{1,0:T(8,128)(2,1)S(1)} %get-tuple-element.30), channel_id=1, source_target_pairs={{0,16},{1,17},{2,18},{3,19},{4,20},{5,21},{6,22},{7,23},{8,24},{9,... | collective-permute-start | bytes 442376 | tf_op jit(solution)/shard_map/ppermute | solution.py:81
  6.5 1.0 slice_bitcast_fusion.19
  7.6 2.9 %collective-permute-start.8 = (bf16[64,1280]{1,0:T(8,128)(2,1)S(1)}, bf16[64,1280]{1,0:T(8,128)(2,1)S(1)}, u32[]{:S(2)}, u32[]{:S(2)}) collective-permute-start(bf16[64,1280]{1,0:T(8,128)(2,1)S(1)} %get-tuple-element.33), channel_id=1, source_target_pairs={{0,16},{1,17},{2,18},{3,19},{4,20},{5,21},{6,22},{7,23},{8,24},{9,... | collective-permute-start | bytes 491528 | tf_op jit(solution)/shard_map/ppermute | solution.py:81
  10.6 9.3 %collective-permute-done.4 = bf16[64,1152]{1,0:T(8,128)(2,1)S(1)} collective-permute-done((bf16[64,1152]{1,0:T(8,128)(2,1)S(1)}, bf16[64,1152]{1,0:T(8,128)(2,1)S(1)}, u32[]{:S(2)}, u32[]{:S(2)}) %collective-permute-start.4) | collective-permute-done | bytes 147488 | tf_op jit(solution)/shard_map/ppermute | solution.py:81
  20.0 3.5 %collective-permute-done = bf16[64,1280]{1,0:T(8,128)(2,1)S(1)} collective-permute-done((bf16[64,1280]{1,0:T(8,128)(2,1)S(1)}, bf16[64,1280]{1,0:T(8,128)(2,1)S(1)}, u32[]{:S(2)}, u32[]{:S(2)}) %collective-permute-start) | collective-permute-done | bytes 163872 | tf_op jit(solution)/shard_map/ppermute | solution.py:81
  23.6 1.9 collective-permute-start.1
  25.5 0.7 collective-permute-done.8
  26.2 1.6 collective-permute-start.9
  27.8 4.6 %collective-permute-done.5 = bf16[2,64,1152]{2,1,0:T(8,128)(2,1)S(1)} collective-permute-done((bf16[2,64,1152]{2,1,0:T(8,128)(2,1)S(1)}, bf16[2,64,1152]{2,1,0:T(8,128)(2,1)S(1)}, u32[]{:S(2)}, u32[]{:S(2)}) %collective-permute-start.5) | collective-permute-done | bytes 294944 | tf_op jit(solution)/shard_map/ppermute | solution.py:81
  32.5 1.6 collective-permute-start.6
  34.2 1.6 collective-permute-start.2
  35.9 1.2 collective-permute-start.10
  37.1 10.7 %collective-permute-done.6 = bf16[2,2,64,1152]{3,2,0,1:T(8,128)(2,1)S(1)} collective-permute-done((bf16[2,2,64,1152]{3,2,0,1:T(8,128)(2,1)S(1)}, bf16[2,2,64,1152]{3,2,0,1:T(8,128)(2,1)S(1)}, u32[]{:S(2)}, u32[]{:S(2)}) %collective-permute-start.6) | collective-permute-done | bytes 589856 | tf_op jit(solution)/shard_map/ppermute | solution.py:81
  48.0 1.6 collective-permute-start.7
  49.6 1.8 collective-permute-done.2
  52.2 1.4 collective-permute-start.11
  53.6 22.4 %collective-permute-done.7 = bf16[2,2,2,64,1152]{4,3,0,1,2:T(8,128)(2,1)S(1)} collective-permute-done((bf16[2,2,2,64,1152]{4,3,0,1,2:T(8,128)(2,1)S(1)}, bf16[2,2,2,64,1152]{4,3,0,1,2:T(8,128)(2,1)S(1)}, u32[]{:S(2)}, u32[]{:S(2)}) %collective-permute-start.7) | collective-permute-done | bytes 1179680 | tf_op jit(solution)/shard_map/ppermute | solution.py:81
  76.4 4.0 %collective-permute-done.3 = bf16[2,2,2,64,1280]{4,3,0,1,2:T(8,128)(2,1)S(1)} collective-permute-done((bf16[2,2,2,64,1280]{4,3,0,1,2:T(8,128)(2,1)S(1)}, bf16[2,2,2,64,1280]{4,3,0,1,2:T(8,128)(2,1)S(1)}, u32[]{:S(2)}, u32[]{:S(2)}) %collective-permute-start.3) | collective-permute-done | bytes 1310752 | tf_op jit(solution)/shard_map/ppermute | solution.py:81
  82.0 3.5 %pad_maximum_fusion.tok_ref = bf16[1024,3712]{1,0:T(8,128)(2,1)} fusion(bf16[1024,1280]{1,0:T(8,128)(2,1)S(1)} %bitcast.133, bf16[1024,1280]{1,0:T(8,128)(2,1)S(1)} %bitcast.135, bf16[1024,1152]{1,0:T(8,128)(2,1)S(1)} %bitcast.138), kind=kLoop, calls=%fused_computation.1 | loop fusion | flops 22806528 | bytes 15204352 | tf_op jit(solution)/shard_map/concatenate | solution.py:95
  86.7 24.1 %reshape_squeeze.6.first_ref = bf16[2,3584,1024]{2,1,0:T(8,128)(2,1)} reshape(bf16[1,2,3584,2,512]{4,3,2,1,0:T(2,128)(2,1)} %param.10) | data formatting | bytes 29360128 | tf_op jit(solution)/shard_map/reshape;squeeze | solution.py:145
  110.8 1.0 slice_convert_fusion
  112.8 0.7 reshape.85.place_ref
  114.2 27.5 %shard_map.65 = bf16[1024,3584]{1,0:T(8,128)(2,1)} custom-call(s32[4,256]{1,0:T(4,128)} %reshape.85.place_ref, f32[4,256]{1,0:T(4,128)} %reshape.86.gate_ref, bf16[1024,3712]{1,0:T(8,128)(2,1)} %collective-permute-done.12.tok_ref, bf16[2,3584,1024]{2,1,0:T(8,128)(2,1)} %reshape_squeeze.6.first_ref, bf16[1024,3584]{1,0:T(8,128)(2,1)} %bitcast.155), custom_call_target="tpu_custom_call" | custom-call | flops 16999999488 | bytes 40000000 | tf_op jit(solution)/shard_map/pallas_call | solution.py:165
  143.2 0.7 reshape.80.place_ref
  144.6 27.4 %shard_map.64 = bf16[1024,3584]{1,0:T(8,128)(2,1)} custom-call(s32[4,256]{1,0:T(4,128)} %reshape.80.place_ref, f32[4,256]{1,0:T(4,128)} %reshape.81.gate_ref, bf16[1024,3712]{1,0:T(8,128)(2,1)} %pad_maximum_fusion.tok_ref, bf16[2,3584,1024]{2,1,0:T(8,128)(2,1)} %reshape_squeeze.6.first_ref, bf16[1024,3584]{1,0:T(8,128)(2,1)} %bitcast.156), custom_call_target="tpu_custom_call" | custom-call | flops 16999999488 | bytes 40000000 | tf_op jit(solution)/shard_map/pallas_call | solution.py:165
  172.0 10.0 %add_convert_fusion = bf16[1024,3584]{1,0:T(8,128)(2,1)} fusion(bf16[1024,3584]{1,0:T(8,128)(2,1)} %collective-permute-done.13, bf16[1024,3584]{1,0:T(8,128)(2,1)} %shard_map.64), kind=kLoop, calls=%fused_computation | loop fusion | flops 14680064 | bytes 22020096 | tf_op jit(solution)/shard_map/convert_element_type | solution.py:193
  182.0 2.7 %fusion.33 = (bf16[1024,1152]{1,0:T(8,128)(2,1)S(1)}, bf16[1024,1152]{1,0:T(8,128)(2,1)S(1)}) fusion(bf16[1024,3584]{1,0:T(8,128)(2,1)} %add_convert_fusion), kind=kLoop, calls=%fused_computation.105 | loop fusion | bytes 9437184 | tf_op jit(solution)/shard_map/slice | solution.py:103
  185.1 1.0 collective-permute-start.14
  186.4 1.4 collective-permute-start.18
  188.2 1.6 collective-permute-start.22
  189.7 23.3 %collective-permute-done.14 = bf16[2,2,2,64,1152]{4,3,0,1,2:T(8,128)(2,1)S(1)} collective-permute-done((bf16[2,2,2,64,1152]{4,3,0,1,2:T(8,128)(2,1)S(1)}, bf16[2,2,2,64,1152]{4,3,0,1,2:T(8,128)(2,1)S(1)}, u32[]{:S(2)}, u32[]{:S(2)}) %collective-permute-start.14) | collective-permute-done | bytes 1179680 | tf_op jit(solution)/shard_map/ppermute | solution.py:81
  213.4 0.8 collective-permute-start.15
  214.6 1.4 collective-permute-start.19
  216.0 3.9 %collective-permute-done.22 = bf16[2,2,2,64,1280]{4,3,0,1,2:T(8,128)(2,1)S(1)} collective-permute-done((bf16[2,2,2,64,1280]{4,3,0,1,2:T(8,128)(2,1)S(1)}, bf16[2,2,2,64,1280]{4,3,0,1,2:T(8,128)(2,1)S(1)}, u32[]{:S(2)}, u32[]{:S(2)}) %collective-permute-start.22) | collective-permute-done | bytes 1310752 | tf_op jit(solution)/shard_map/ppermute | solution.py:81
  220.3 1.2 collective-permute-start.23
  221.5 6.4 %collective-permute-done.15 = bf16[2,2,64,1152]{3,2,0,1:T(8,128)(2,1)S(1)} collective-permute-done((bf16[2,2,64,1152]{3,2,0,1:T(8,128)(2,1)S(1)}, bf16[2,2,64,1152]{3,2,0,1:T(8,128)(2,1)S(1)}, u32[]{:S(2)}, u32[]{:S(2)}) %collective-permute-start.15) | collective-permute-done | bytes 589856 | tf_op jit(solution)/shard_map/ppermute | solution.py:81
  228.1 1.0 collective-permute-start.16
  229.1 3.4 %collective-permute-done.19 = bf16[2,2,64,1152]{3,2,0,1:T(8,128)(2,1)S(1)} collective-permute-done((bf16[2,2,64,1152]{3,2,0,1:T(8,128)(2,1)S(1)}, bf16[2,2,64,1152]{3,2,0,1:T(8,128)(2,1)S(1)}, u32[]{:S(2)}, u32[]{:S(2)}) %collective-permute-start.19) | collective-permute-done | bytes 589856 | tf_op jit(solution)/shard_map/ppermute | solution.py:81
  232.7 1.2 collective-permute-start.20
  233.9 2.2 collective-permute-done.23
  236.3 1.4 collective-permute-start.24
  237.8 3.5 %collective-permute-start.17 = (bf16[64,1152]{1,0:T(8,128)(2,1)S(1)}, bf16[64,1152]{1,0:T(8,128)(2,1)S(1)}, u32[]{:S(2)}, u32[]{:S(2)}) collective-permute-start(bf16[64,1152]{1,0:T(8,128)(2,1)S(1)} %slice_bitcast_fusion.16), channel_id=1, source_target_pairs={{0,16},{1,17},{2,18},{3,19},{4,20},{5,21},{6,22},{7,23},{8,24},{9,... | collective-permute-start | bytes 442376 | tf_op jit(solution)/shard_map/ppermute | solution.py:81
  241.4 3.2 %collective-permute-start.21 = (bf16[64,1152]{1,0:T(8,128)(2,1)S(1)}, bf16[64,1152]{1,0:T(8,128)(2,1)S(1)}, u32[]{:S(2)}, u32[]{:S(2)}) collective-permute-start(bf16[64,1152]{1,0:T(8,128)(2,1)S(1)} %slice_bitcast_fusion.14), channel_id=1, source_target_pairs={{0,16},{1,17},{2,18},{3,19},{4,20},{5,21},{6,22},{7,23},{8,24},{9,... | collective-permute-start | bytes 442376 | tf_op jit(solution)/shard_map/ppermute | solution.py:81
  244.6 6.1 %collective-permute-done.17 = bf16[64,1152]{1,0:T(8,128)(2,1)S(1)} collective-permute-done((bf16[64,1152]{1,0:T(8,128)(2,1)S(1)}, bf16[64,1152]{1,0:T(8,128)(2,1)S(1)}, u32[]{:S(2)}, u32[]{:S(2)}) %collective-permute-start.17) | collective-permute-done | bytes 147488 | tf_op jit(solution)/shard_map/ppermute | solution.py:81
  251.0 4.7 %collective-permute-done.21 = bf16[64,1152]{1,0:T(8,128)(2,1)S(1)} collective-permute-done((bf16[64,1152]{1,0:T(8,128)(2,1)S(1)}, bf16[64,1152]{1,0:T(8,128)(2,1)S(1)}, u32[]{:S(2)}, u32[]{:S(2)}) %collective-permute-start.21) | collective-permute-done | bytes 147488 | tf_op jit(solution)/shard_map/ppermute | solution.py:81
  255.7 5.0 %collective-permute-done.25 = bf16[64,1280]{1,0:T(8,128)(2,1)S(1)} collective-permute-done((bf16[64,1280]{1,0:T(8,128)(2,1)S(1)}, bf16[64,1280]{1,0:T(8,128)(2,1)S(1)}, u32[]{:S(2)}, u32[]{:S(2)}) %collective-permute-start.25) | collective-permute-done | bytes 163872 | tf_op jit(solution)/shard_map/ppermute | solution.py:81
  260.7 0.8 pad_maximum_fusion.10
  (79 shorter events, 12.5 us)
Async XLA Ops:
  0.9 19.0 %collective-permute-start.4 = (bf16[64,1152]{1,0:T(8,128)(2,1)S(1)}, bf16[64,1152]{1,0:T(8,128)(2,1)S(1)}, u32[]{:S(2)}, u32[]{:S(2)}) collective-permute-start(bf16[64,1152]{1,0:T(8,128)(2,1)S(1)} %get-tuple-element.30), channel_id=1, source_target_pairs={{0,16},{1,17},{2,18},{3,19},{4,20},{5,21},{6,22},{7,23},{8,24},{9,... | collective-permute-start | bytes 442376 | tf_op jit(solution)/shard_map/ppermute | solution.py:81
  7.6 15.9 %collective-permute-start = (bf16[64,1280]{1,0:T(8,128)(2,1)S(1)}, bf16[64,1280]{1,0:T(8,128)(2,1)S(1)}, u32[]{:S(2)}, u32[]{:S(2)}) collective-permute-start(bf16[64,1280]{1,0:T(8,128)(2,1)S(1)} %get-tuple-element.32), channel_id=1, source_target_pairs={{0,16},{1,17},{2,18},{3,19},{4,20},{5,21},{6,22},{7,23},{8,24},{9,... | collective-permute-start | bytes 491528 | tf_op jit(solution)/shard_map/ppermute | solution.py:81
  7.6 18.5 %collective-permute-start.8 = (bf16[64,1280]{1,0:T(8,128)(2,1)S(1)}, bf16[64,1280]{1,0:T(8,128)(2,1)S(1)}, u32[]{:S(2)}, u32[]{:S(2)}) collective-permute-start(bf16[64,1280]{1,0:T(8,128)(2,1)S(1)} %get-tuple-element.33), channel_id=1, source_target_pairs={{0,16},{1,17},{2,18},{3,19},{4,20},{5,21},{6,22},{7,23},{8,24},{9,... | collective-permute-start | bytes 491528 | tf_op jit(solution)/shard_map/ppermute | solution.py:81
  19.9 12.5 %collective-permute-start.5 = (bf16[2,64,1152]{2,1,0:T(8,128)(2,1)S(1)}, bf16[2,64,1152]{2,1,0:T(8,128)(2,1)S(1)}, u32[]{:S(2)}, u32[]{:S(2)}) collective-permute-start(bf16[2,64,1152]{2,1,0:T(8,128)(2,1)S(1)} %get-tuple-element.39), channel_id=1, source_target_pairs={{0,8},{1,9},{2,10},{3,11},{4,12},{5,13},{6,14},{7,15},{8,0},{9,1},... | collective-permute-start | bytes 884744 | tf_op jit(solution)/shard_map/ppermute | solution.py:81
  23.6 10.6 %collective-permute-start.1 = (bf16[2,64,1280]{2,1,0:T(8,128)(2,1)S(1)}, bf16[2,64,1280]{2,1,0:T(8,128)(2,1)S(1)}, u32[]{:S(2)}, u32[]{:S(2)}) collective-permute-start(bf16[2,64,1280]{2,1,0:T(8,128)(2,1)S(1)} %get-tuple-element.37), channel_id=1, source_target_pairs={{0,4},{1,5},{2,6},{3,7},{4,0},{5,1},{6,2},{7,3},{8,12},{9,13},{10,... | collective-permute-start | bytes 983048 | tf_op jit(solution)/shard_map/ppermute | solution.py:81
  26.2 9.5 %collective-permute-start.9 = (bf16[2,64,1280]{2,1,0:T(8,128)(2,1)S(1)}, bf16[2,64,1280]{2,1,0:T(8,128)(2,1)S(1)}, u32[]{:S(2)}, u32[]{:S(2)}) collective-permute-start(bf16[2,64,1280]{2,1,0:T(8,128)(2,1)S(1)} %get-tuple-element.35), channel_id=1, source_target_pairs={{0,2},{1,3},{2,0},{3,1},{4,6},{5,7},{6,4},{7,5},{8,10},{9,11},{10,... | collective-permute-start | bytes 983048 | tf_op jit(solution)/shard_map/ppermute | solution.py:81
  32.5 15.3 %collective-permute-start.6 = (bf16[2,2,64,1152]{3,2,0,1:T(8,128)(2,1)S(1)}, bf16[2,2,64,1152]{3,2,0,1:T(8,128)(2,1)S(1)}, u32[]{:S(2)}, u32[]{:S(2)}) collective-permute-start(bf16[2,2,64,1152]{3,2,0,1:T(8,128)(2,1)S(1)} %get-tuple-element.28), channel_id=1, source_target_pairs={{0,4},{1,5},{2,6},{3,7},{4,0},{5,1},{6,2},{7,3},{8,12},{9,13},{10,... | collective-permute-start | bytes 1769480 | tf_op jit(solution)/shard_map/ppermute | solution.py:81
  34.2 17.2 %collective-permute-start.2 = (bf16[2,2,64,1280]{3,2,0,1:T(8,128)(2,1)S(1)}, bf16[2,2,64,1280]{3,2,0,1:T(8,128)(2,1)S(1)}, u32[]{:S(2)}, u32[]{:S(2)}) collective-permute-start(bf16[2,2,64,1280]{3,2,0,1:T(8,128)(2,1)S(1)} %get-tuple-element.26), channel_id=1, source_target_pairs={{0,2},{1,3},{2,0},{3,1},{4,6},{5,7},{6,4},{7,5},{8,10},{9,11},{10,... | collective-permute-start | bytes 1966088 | tf_op jit(solution)/shard_map/ppermute | solution.py:81
  35.9 16.2 %collective-permute-start.10 = (bf16[2,2,64,1280]{3,2,0,1:T(8,128)(2,1)S(1)}, bf16[2,2,64,1280]{3,2,0,1:T(8,128)(2,1)S(1)}, u32[]{:S(2)}, u32[]{:S(2)}) collective-permute-start(bf16[2,2,64,1280]{3,2,0,1:T(8,128)(2,1)S(1)} %get-tuple-element.24), channel_id=1, source_target_pairs={{0,8},{1,9},{2,10},{3,11},{4,12},{5,13},{6,14},{7,15},{8,0},{9,1},... | collective-permute-start | bytes 1966088 | tf_op jit(solution)/shard_map/ppermute | solution.py:81
  48.0 28.0 %collective-permute-start.7 = (bf16[2,2,2,64,1152]{4,3,0,1,2:T(8,128)(2,1)S(1)}, bf16[2,2,2,64,1152]{4,3,0,1,2:T(8,128)(2,1)S(1)}, u32[]{:S(2)}, u32[]{:S(2)}) collective-permute-start(bf16[2,2,2,64,1152]{4,3,0,1,2:T(8,128)(2,1)S(1)} %get-tuple-element.22), channel_id=1, source_target_pairs={{0,2},{1,3},{2,0},{3,1},{4,6},{5,7},{6,4},{7,5},{8,10},{9,11},{10,... | collective-permute-start | bytes 3538952 | tf_op jit(solution)/shard_map/ppermute | solution.py:81
  51.6 28.8 %collective-permute-start.3 = (bf16[2,2,2,64,1280]{4,3,0,1,2:T(8,128)(2,1)S(1)}, bf16[2,2,2,64,1280]{4,3,0,1,2:T(8,128)(2,1)S(1)}, u32[]{:S(2)}, u32[]{:S(2)}) collective-permute-start(bf16[2,2,2,64,1280]{4,3,0,1,2:T(8,128)(2,1)S(1)} %get-tuple-element.20), channel_id=1, source_target_pairs={{0,8},{1,9},{2,10},{3,11},{4,12},{5,13},{6,14},{7,15},{8,0},{9,1},... | collective-permute-start | bytes 3932168 | tf_op jit(solution)/shard_map/ppermute | solution.py:81
  52.2 29.3 %collective-permute-start.11 = (bf16[2,2,2,64,1280]{4,3,0,2,1:T(8,128)(2,1)S(1)}, bf16[2,2,2,64,1280]{4,3,0,2,1:T(8,128)(2,1)S(1)}, u32[]{:S(2)}, u32[]{:S(2)}) collective-permute-start(bf16[2,2,2,64,1280]{4,3,0,2,1:T(8,128)(2,1)S(1)} %get-tuple-element.18), channel_id=1, source_target_pairs={{0,4},{1,5},{2,6},{3,7},{4,0},{5,1},{6,2},{7,3},{8,12},{9,13},{10,... | collective-permute-start | bytes 3932168 | tf_op jit(solution)/shard_map/ppermute | solution.py:81
  82.0 3.5 %copy-start = (s32[32]{0:T(128)S(1)}, s32[32]{0:T(128)}, u32[]{:S(2)}) copy-start(s32[32]{0:T(128)} %param.9) | copy-start | bytes 388
  85.5 25.3 %collective-permute-start.12 = (bf16[1024,3712]{1,0:T(8,128)(2,1)}, bf16[1024,3712]{1,0:T(8,128)(2,1)}, u32[]{:S(2)}, u32[]{:S(2)}) collective-permute-start(bf16[1024,3712]{1,0:T(8,128)(2,1)} %pad_maximum_fusion.tok_ref), channel_id=1, source_target_pairs={{0,1},{1,0},{2,3},{3,2},{4,5},{5,4},{6,7},{7,6},{8,9},{9,8},{10,11... | collective-permute-start | bytes 22806536 | tf_op jit(solution)/shard_map/ppermute | solution.py:142
  141.6 30.3 %collective-permute-start.13 = (bf16[1024,3584]{1,0:T(8,128)(2,1)}, bf16[1024,3584]{1,0:T(8,128)(2,1)}, u32[]{:S(2)}, u32[]{:S(2)}) collective-permute-start(bf16[1024,3584]{1,0:T(8,128)(2,1)} %shard_map.65), channel_id=1, source_target_pairs={{0,1},{1,0},{2,3},{3,2},{4,5},{5,4},{6,7},{7,6},{8,9},{9,8},{10,11... | collective-permute-start | bytes 22020104 | tf_op jit(solution)/shard_map/ppermute | solution.py:192
  185.1 28.0 %collective-permute-start.14 = (bf16[2,2,2,64,1152]{4,3,0,1,2:T(8,128)(2,1)S(1)}, bf16[2,2,2,64,1152]{4,3,0,1,2:T(8,128)(2,1)S(1)}, u32[]{:S(2)}, u32[]{:S(2)}) collective-permute-start(bf16[2,2,2,64,1152]{4,3,0,1,2:T(8,128)(2,1)S(1)} %bitcast.143), channel_id=1, source_target_pairs={{0,2},{1,3},{2,0},{3,1},{4,6},{5,7},{6,4},{7,5},{8,10},{9,11},{10,... | collective-permute-start | bytes 3538952 | tf_op jit(solution)/shard_map/ppermute | solution.py:81
  186.1 1.7 slice-start
  186.4 27.8 %collective-permute-start.18 = (bf16[2,2,2,64,1152]{4,3,0,2,1:T(8,128)(2,1)S(1)}, bf16[2,2,2,64,1152]{4,3,0,2,1:T(8,128)(2,1)S(1)}, u32[]{:S(2)}, u32[]{:S(2)}) collective-permute-start(bf16[2,2,2,64,1152]{4,3,0,2,1:T(8,128)(2,1)S(1)} %bitcast.142), channel_id=1, source_target_pairs={{0,4},{1,5},{2,6},{3,7},{4,0},{5,1},{6,2},{7,3},{8,12},{9,13},{10,... | collective-permute-start | bytes 3538952 | tf_op jit(solution)/shard_map/ppermute | solution.py:81
  188.2 31.7 %collective-permute-start.22 = (bf16[2,2,2,64,1280]{4,3,0,1,2:T(8,128)(2,1)S(1)}, bf16[2,2,2,64,1280]{4,3,0,1,2:T(8,128)(2,1)S(1)}, u32[]{:S(2)}, u32[]{:S(2)}) collective-permute-start(bf16[2,2,2,64,1280]{4,3,0,1,2:T(8,128)(2,1)S(1)} %bitcast.141), channel_id=1, source_target_pairs={{0,8},{1,9},{2,10},{3,11},{4,12},{5,13},{6,14},{7,15},{8,0},{9,1},... | collective-permute-start | bytes 3932168 | tf_op jit(solution)/shard_map/ppermute | solution.py:81
  213.4 14.5 %collective-permute-start.15 = (bf16[2,2,64,1152]{3,2,0,1:T(8,128)(2,1)S(1)}, bf16[2,2,64,1152]{3,2,0,1:T(8,128)(2,1)S(1)}, u32[]{:S(2)}, u32[]{:S(2)}) collective-permute-start(bf16[2,2,64,1152]{3,2,0,1:T(8,128)(2,1)S(1)} %slice_bitcast_fusion.4), channel_id=1, source_target_pairs={{0,4},{1,5},{2,6},{3,7},{4,0},{5,1},{6,2},{7,3},{8,12},{9,13},{10,... | collective-permute-start | bytes 1769480 | tf_op jit(solution)/shard_map/ppermute | solution.py:81
  214.6 18.0 %collective-permute-start.19 = (bf16[2,2,64,1152]{3,2,0,1:T(8,128)(2,1)S(1)}, bf16[2,2,64,1152]{3,2,0,1:T(8,128)(2,1)S(1)}, u32[]{:S(2)}, u32[]{:S(2)}) collective-permute-start(bf16[2,2,64,1152]{3,2,0,1:T(8,128)(2,1)S(1)} %slice_bitcast_fusion.2), channel_id=1, source_target_pairs={{0,8},{1,9},{2,10},{3,11},{4,12},{5,13},{6,14},{7,15},{8,0},{9,1},... | collective-permute-start | bytes 1769480 | tf_op jit(solution)/shard_map/ppermute | solution.py:81
  220.3 15.8 %collective-permute-start.23 = (bf16[2,2,64,1280]{3,2,0,1:T(8,128)(2,1)S(1)}, bf16[2,2,64,1280]{3,2,0,1:T(8,128)(2,1)S(1)}, u32[]{:S(2)}, u32[]{:S(2)}) collective-permute-start(bf16[2,2,64,1280]{3,2,0,1:T(8,128)(2,1)S(1)} %slice_bitcast_fusion), channel_id=1, source_target_pairs={{0,2},{1,3},{2,0},{3,1},{4,6},{5,7},{6,4},{7,5},{8,10},{9,11},{10,... | collective-permute-start | bytes 1966088 | tf_op jit(solution)/shard_map/ppermute | solution.py:81
  228.1 9.6 %collective-permute-start.16 = (bf16[2,64,1152]{2,1,0:T(8,128)(2,1)S(1)}, bf16[2,64,1152]{2,1,0:T(8,128)(2,1)S(1)}, u32[]{:S(2)}, u32[]{:S(2)}) collective-permute-start(bf16[2,64,1152]{2,1,0:T(8,128)(2,1)S(1)} %slice_bitcast_fusion.10), channel_id=1, source_target_pairs={{0,8},{1,9},{2,10},{3,11},{4,12},{5,13},{6,14},{7,15},{8,0},{9,1},... | collective-permute-start | bytes 884744 | tf_op jit(solution)/shard_map/ppermute | solution.py:81
  232.7 8.6 %collective-permute-start.20 = (bf16[2,64,1152]{2,1,0:T(8,128)(2,1)S(1)}, bf16[2,64,1152]{2,1,0:T(8,128)(2,1)S(1)}, u32[]{:S(2)}, u32[]{:S(2)}) collective-permute-start(bf16[2,64,1152]{2,1,0:T(8,128)(2,1)S(1)} %slice_bitcast_fusion.8), channel_id=1, source_target_pairs={{0,2},{1,3},{2,0},{3,1},{4,6},{5,7},{6,4},{7,5},{8,10},{9,11},{10,... | collective-permute-start | bytes 884744 | tf_op jit(solution)/shard_map/ppermute | solution.py:81
  236.3 14.5 %collective-permute-start.24 = (bf16[2,64,1280]{2,1,0:T(8,128)(2,1)S(1)}, bf16[2,64,1280]{2,1,0:T(8,128)(2,1)S(1)}, u32[]{:S(2)}, u32[]{:S(2)}) collective-permute-start(bf16[2,64,1280]{2,1,0:T(8,128)(2,1)S(1)} %slice_bitcast_fusion.6), channel_id=1, source_target_pairs={{0,4},{1,5},{2,6},{3,7},{4,0},{5,1},{6,2},{7,3},{8,12},{9,13},{10,... | collective-permute-start | bytes 983048 | tf_op jit(solution)/shard_map/ppermute | solution.py:81
  237.8 13.0 %collective-permute-start.17 = (bf16[64,1152]{1,0:T(8,128)(2,1)S(1)}, bf16[64,1152]{1,0:T(8,128)(2,1)S(1)}, u32[]{:S(2)}, u32[]{:S(2)}) collective-permute-start(bf16[64,1152]{1,0:T(8,128)(2,1)S(1)} %slice_bitcast_fusion.16), channel_id=1, source_target_pairs={{0,16},{1,17},{2,18},{3,19},{4,20},{5,21},{6,22},{7,23},{8,24},{9,... | collective-permute-start | bytes 442376 | tf_op jit(solution)/shard_map/ppermute | solution.py:81
  241.4 14.3 %collective-permute-start.21 = (bf16[64,1152]{1,0:T(8,128)(2,1)S(1)}, bf16[64,1152]{1,0:T(8,128)(2,1)S(1)}, u32[]{:S(2)}, u32[]{:S(2)}) collective-permute-start(bf16[64,1152]{1,0:T(8,128)(2,1)S(1)} %slice_bitcast_fusion.14), channel_id=1, source_target_pairs={{0,16},{1,17},{2,18},{3,19},{4,20},{5,21},{6,22},{7,23},{8,24},{9,... | collective-permute-start | bytes 442376 | tf_op jit(solution)/shard_map/ppermute | solution.py:81
  250.9 9.8 %collective-permute-start.25 = (bf16[64,1280]{1,0:T(8,128)(2,1)S(1)}, bf16[64,1280]{1,0:T(8,128)(2,1)S(1)}, u32[]{:S(2)}, u32[]{:S(2)}) collective-permute-start(bf16[64,1280]{1,0:T(8,128)(2,1)S(1)} %slice_bitcast_fusion.12), channel_id=1, source_target_pairs={{0,16},{1,17},{2,18},{3,19},{4,20},{5,21},{6,22},{7,23},{8,24},{9,... | collective-permute-start | bytes 491528 | tf_op jit(solution)/shard_map/ppermute | solution.py:81
